TPU v7x, 32 devices: a whole 2x2x4 slice. The times are simulated.
32 devices in a mesh: req: 16 (over z, y, x), tp: 2 (over core).
Axes of the slice: x: 2, y: 2, z: 4, core: 2. Of those that a mesh axis runs over, the one named last changes fastest.
Arguments:
- residual: bfloat16 [512, 2048], P('req'), may hold values from -6 to 6
- fresh_qkv: bfloat16 [512, 3, 2048], P('req', None, 'tp'), may hold values from -32 to 32
- kv_cache: bfloat16 [512, 24, 2, 2048], P('req', None, None, 'tp'), may hold values from -32 to 32
- cache_len: int32 [512], P('req'), may hold values from 2 to 24, as said below
- out_proj: bfloat16 [2048, 2048], P('tp'), may hold values from -0.125 to 0.125
- norm_gain: float32 [2048], replicated, may hold values from 0.1 to 1.9
- router_weight: float32 [2048, 16], replicated, may hold values from -7.9549513 to 7.9549513
- expert_ids: int32 [512, 8], P('req'), may hold values from 0 to 15, all different within a row; in each aligned block of 32 rows (0 to 31, 32 to 63, ...) at most 32 rows name the same one
- gate_up: bfloat16 [16, 2048, 2, 1024], P('req', None, None, 'tp'), may hold values from -0.125 to 0.125
- down_proj: bfloat16 [16, 1024, 2048], P('req', 'tp'), may hold values from -0.1875 to 0.1875
Outputs:
- layer_out: bfloat16 [512, 2048], P('req', 'tp')
Inputs may be any that keep to these rules, and one draw needn't show every extreme that they name: `expert_ids`: each row names 8 different experts; among the 32 rows of one device no expert is named by more than 32 rows, and some device reaches 32. `cache_len`: some request uses all 24 positions.
All inputs are finite; a program needn't handle non-finite values.
Results may differ from a plain program's by a relative error of at most 0.018.
Values may be sent and summed in bfloat16 or wider, within the bound.
A program may use at most 128 MiB of HBM per device.

v0:
```python
import jax
import jax.numpy as jnp
from jax import lax
from jax.sharding import PartitionSpec as P

HD = 128


def rms_normed(hidden_in, gain):
    values = hidden_in.astype(jnp.float32)
    scale_inv = lax.rsqrt(jnp.mean(values * values, axis=-1, keepdims=True) + 1e-05)
    return (values * scale_inv * gain).astype(jnp.bfloat16)


def attend(fresh_qkv, kv_cache, cache_len):
    requests, ctx_len = (kv_cache.shape[0], kv_cache.shape[1])
    local_heads = fresh_qkv.shape[2] // HD
    queries = fresh_qkv[:, 0].reshape(requests, local_heads, HD)
    new_keys = fresh_qkv[:, 1].reshape(requests, local_heads, HD)
    new_values = fresh_qkv[:, 2].reshape(requests, local_heads, HD)
    cache_keys = kv_cache[:, :, 0].reshape(requests, ctx_len, local_heads, HD)
    cache_values = kv_cache[:, :, 1].reshape(requests, ctx_len, local_heads, HD)
    factor = HD ** (-0.5)
    scores = (
        jnp.einsum("nhd,nchd->nhc", queries, cache_keys, preferred_element_type=jnp.float32)
        * factor
    )
    own_score = (
        jnp.einsum("nhd,nhd->nh", queries, new_keys, preferred_element_type=jnp.float32) * factor
    )
    valid = (jnp.arange(ctx_len, dtype=jnp.int32)[None, :] < cache_len[:, None])[:, None, :]
    masked = jnp.where(valid, scores, -jnp.inf)
    top_score = jnp.maximum(jnp.max(masked, axis=-1), own_score)
    expos = jnp.where(valid, jnp.exp(masked - top_score[..., None]), 0.0)
    own_expo = jnp.exp(own_score - top_score)
    total = jnp.sum(expos, axis=-1) + own_expo
    weights = (expos / total[..., None]).astype(jnp.bfloat16)
    own_weight = (own_expo / total).astype(jnp.bfloat16)
    mixed = jnp.einsum("nhc,nchd->nhd", weights, cache_values, preferred_element_type=jnp.float32)
    mixed = mixed + own_weight.astype(jnp.float32)[..., None] * new_values.astype(jnp.float32)
    return mixed.astype(jnp.bfloat16).reshape(requests, local_heads * HD)


def local(
    residual,
    fresh_qkv,
    kv_cache,
    cache_len,
    out_proj,
    norm_gain,
    router_weight,
    expert_ids,
    gate_up,
    down_proj,
):
    tp_place = lax.axis_index("tp")
    me = lax.axis_index("req")
    experts = lax.axis_size("req")
    attended = attend(fresh_qkv, kv_cache, cache_len)
    partial_value = jnp.dot(attended, out_proj, preferred_element_type=jnp.float32)
    summed = lax.psum(partial_value, "tp")
    hidden = (residual.astype(jnp.float32) + summed).astype(jnp.bfloat16)
    normed = rms_normed(hidden, norm_gain)
    rows = lax.all_gather(normed, "req", axis=0, tiled=True)
    logits = jnp.dot(normed.astype(jnp.float32), router_weight, precision=lax.Precision.HIGHEST)
    named = jnp.any(
        expert_ids[:, :, None] == jnp.arange(experts, dtype=jnp.int32)[None, None, :], axis=1
    )
    gates = jax.nn.softmax(jnp.where(named, logits, -jnp.inf), axis=-1)
    gates_all = lax.all_gather(gates, "req", axis=0, tiled=True)
    mine = jnp.arange(experts, dtype=jnp.int32)[None, :] == me
    weight = jnp.sum(jnp.where(mine, gates_all, 0.0), axis=1, keepdims=True)
    gate_part = jnp.dot(rows, gate_up[0, :, 0], preferred_element_type=jnp.float32)
    up_part = jnp.dot(rows, gate_up[0, :, 1], preferred_element_type=jnp.float32)
    inner = (jax.nn.silu(gate_part) * up_part).astype(jnp.bfloat16)
    result = jnp.dot(inner, down_proj[0], preferred_element_type=jnp.float32)
    own = lax.psum_scatter(result * weight, "tp", scatter_dimension=1, tiled=True)
    moe_share = lax.psum_scatter(own, "req", scatter_dimension=0, tiled=True)
    width_here = moe_share.shape[1]
    own_cols = lax.dynamic_slice_in_dim(hidden, tp_place * width_here, width_here, 1)
    return (own_cols.astype(jnp.float32) + moe_share).astype(jnp.bfloat16)


def solution(mesh):
    in_specs = (
        P("req", None),
        P("req", None, "tp"),
        P("req", None, None, "tp"),
        P("req"),
        P("tp", None),
        P(),
        P(),
        P("req", None),
        P("req", None, None, "tp"),
        P("req", "tp", None),
    )
    out_specs = P("req", "tp")
    return jax.shard_map(local, mesh=mesh, in_specs=in_specs, out_specs=out_specs, check_vma=False)
```

profile of v0, /device:TPU:0, one launch (start us, length us, event | category | flops | bytes accessed | tf_op | source)
XLA Modules:
  0.0 234.0 jit_solution(13227113264910571109)
XLA Ops:
  6.5 0.8 iota_compare_fusion.1
  7.4 0.9 convert_bitcast_fusion
  8.4 0.1 fusion.20
  8.5 0.1 copy.30
  8.5 0.1 reshape.54
  8.6 17.1 %slice_reduce_fusion = (bf16[32,24,1024]{2,1,0:T(8,128)(2,1)}, bf16[32,24,1024]{2,1,0:T(8,128)(2,1)S(1)}) fusion(bf16[32,24,2,1024]{3,2,1,0:T(2,128)(2,1)} %param.12), kind=kLoop, calls=%fused_computation.1 | loop fusion | bytes 6291456 | tf_op jit(solution)/shard_map/slice | solution.py:22
  25.7 0.9 fusion.6
  26.7 0.1 copy.26
  26.9 0.1 copy.20
  27.0 0.2 copy.31
  27.2 2.0 fusion.3
  29.2 0.1 fusion.19
  29.3 3.8 %fusion.24 = f32[32,2048]{1,0:T(8,128)} fusion(bf16[1024,2048]{1,0:T(8,128)(2,1)} %param.14, bf16[4,8,8,128]{3,2,1,0:T(8,128)(2,1)S(1)} %bitcast.84), kind=kOutput, calls=%fused_computation.40 | convolution fusion | flops 134217728 | bytes 4521984 | tf_op jit(solution)/shard_map/dot_general | solution.py:60
  33.1 0.0 all-reduce.2.cloned.1.call-update
  33.1 0.0 all-gather.3.cloned.1.call-start
  33.2 21.1 %all-reduce.2.cloned.1.call-done = f32[32,2048]{1,0:T(8,128)} async-done(((f32[32,2048]{1,0:T(8,128)}), f32[32,2048]{1,0:T(8,128)}) %all-reduce.2.cloned.1.call-update) | async-done | bytes 262160 | tf_op jit(solution)/shard_map/psum | solution.py:61
  54.3 1.1 fusion.15
  55.4 0.7 fusion.17
  56.1 0.0 all-gather.3.cloned.1.call-update
  56.1 0.0 reduce-scatter.3.cloned.1.call-start
  56.3 10.4 %fusion.33 = (bf16[1,2048,1,512]{3,2,1,0:T(2,128)(2,1)}, bf16[1,2048,1,512]{3,2,1,0:T(2,128)(2,1)}) fusion(bf16[1,2048,2,512]{3,2,1,0:T(2,128)(2,1)} %param.18), kind=kLoop, calls=%fused_computation.61 | loop fusion | bytes 8388608 | tf_op jit(solution)/shard_map/slice | solution.py:73
  66.7 0.2 fusion.34
  67.0 41.8 %all-gather = f32[16,32,16]{1,2,0:T(8,128)S(1)} all-gather(f32[1,32,16]{1,2,0:T(8,128)S(1)} %divide_bitcast_fusion), channel_id=1, replica_groups=mesh['req'=16,'tp'=2] {'req'}, dimensions={0}, use_global_device_ids=true | all-gather | bytes 34816 | tf_op jit(solution)/shard_map/all_gather | solution.py:70
  108.9 0.1 reshape.46
  109.0 0.1 select_reduce_fusion
  109.1 10.6 %all-gather.3.cloned.1.call-done = bf16[512,2048]{1,0:T(8,128)(2,1)} async-done(((bf16[32,2048]{1,0:T(8,128)(2,1)}), bf16[512,2048]{1,0:T(8,128)(2,1)}) %all-gather.3.cloned.1.call-update) | async-done | bytes 2097168 | tf_op jit(solution)/shard_map/all_gather | solution.py:64
  119.6 4.1 %fusion.1 = f32[512,512]{1,0:T(8,128)S(1)} fusion(bf16[512,2048]{1,0:T(8,128)(2,1)} %all-gather.3.cloned.1.call-done, bf16[1,2048,1,512]{3,2,1,0:T(2,128)(2,1)} %get-tuple-element.9), kind=kOutput, calls=%fused_computation.6 | convolution fusion | flops 1073741824 | bytes 5242880 | tf_op jit(solution)/shard_map/dot_general | solution.py:73
  123.7 7.3 %convolution_multiply_fusion = f32[512,2048]{1,0:T(8,128)} fusion(bf16[1,512,2048]{2,1,0:T(8,128)(2,1)S(1)} %copy-done, f32[512]{0:T(512)S(1)} %select_reduce_fusion, bf16[512,2048]{1,0:T(8,128)(2,1)} %all-gather.3.cloned.1.call-done, bf16[1,2048,1,512]{3,2,1,0:T(2,128)(2,1)} %get-tuple-element.10, f32[512,512]{1,0:T(8,128)S(1)} %fusion.1), kind=kOutput, calls=%fused_computation | convolution fusion | flops 2150105088 | bytes 11536384 | tf_op jit(solution)/shard_map/dot_general | solution.py:76
  131.0 0.0 reduce-scatter.5.cloned.1.call-start
  131.1 10.8 %reduce-scatter.3.cloned.1.call-done = f32[512,1024]{1,0:T(8,128)} async-done(((f32[512,2048]{1,0:T(8,128)}), f32[512,1024]{1,0:T(8,128)}) %reduce-scatter.3.cloned.1.call-update) | async-done | bytes 2097168 | tf_op jit(solution)/shard_map/reduce_scatter | solution.py:77
  141.9 84.1 %reduce-scatter.5.cloned.1.call-done = f32[32,1024]{1,0:T(8,128)} async-done(((f32[512,1024]{1,0:T(8,128)}), f32[32,1024]{1,0:T(8,128)}) %reduce-scatter.5.cloned.1.call-update) | async-done | bytes 131088 | tf_op jit(solution)/shard_map/reduce_scatter | solution.py:78
  226.0 1.5 add_convert_fusion.1
  (29 shorter events, 0.4 us)
Async XLA Ops:
  6.5 117.2 %copy-start = (bf16[1,512,2048]{2,1,0:T(8,128)(2,1)S(1)}, bf16[1,512,2048]{2,1,0:T(8,128)(2,1)}, u32[]{:S(2)}) copy-start(bf16[1,512,2048]{2,1,0:T(8,128)(2,1)} %param.19) | copy-start | bytes 6291460
  6.5 47.7 %all-reduce.2.cloned.1.call-start = ((), (), s32[]{:S(2)}) async-start(), calls=%async_computation.2 | async-start | bytes 524288 | tf_op jit(solution)/shard_map/psum | solution.py:61
  29.3 25.0 %copy-start.2 = (bf16[32,2048]{1,0:T(8,128)(2,1)S(1)}, bf16[32,2048]{1,0:T(8,128)(2,1)}, u32[]{:S(2)}) copy-start(bf16[32,2048]{1,0:T(8,128)(2,1)} %param.10) | copy-start | bytes 393220
  29.3 26.1 %copy-start.4 = (f32[2048]{0:T(1024)S(1)}, f32[2048]{0:T(1024)}, u32[]{:S(2)}) copy-start(f32[2048]{0:T(1024)} %param.15) | copy-start | bytes 24580
  29.3 26.9 %copy-start.5 = (s32[32,8]{0,1:T(8,128)S(1)}, s32[32,8]{0,1:T(8,128)}, u32[]{:S(2)}) copy-start(s32[32,8]{0,1:T(8,128)} %param.17) | copy-start | bytes 3076
  33.1 86.5 %all-gather.3.cloned.1.call-start = ((), (), s32[]{:S(2)}) async-start(), calls=%async_computation.3 | async-start | bytes 2228224 | tf_op jit(solution)/shard_map/all_gather | solution.py:64
  56.1 85.7 %reduce-scatter.3.cloned.1.call-start = ((), (), s32[]{:S(2)}) async-start(), calls=%async_computation.4 | async-start | bytes 6291456 | tf_op jit(solution)/shard_map/reduce_scatter | solution.py:77
  56.2 10.5 %copy-start.1 = (bf16[32,2048]{1,0:T(8,128)(2,1)S(1)}, bf16[32,2048]{1,0:T(8,128)(2,1)}, u32[]{:S(2)}) copy-start(bf16[32,2048]{1,0:T(8,128)(2,1)} %fusion.17) | copy-start | bytes 393220
  56.3 10.5 %copy-start.3 = (f32[2048,16]{0,1:T(8,128)S(1)}, f32[2048,16]{0,1:T(8,128)}, u32[]{:S(2)}) copy-start(f32[2048,16]{0,1:T(8,128)} %param.16) | copy-start | bytes 393220
  131.0 95.0 %reduce-scatter.5.cloned.1.call-start = ((), (), s32[]{:S(2)}) async-start(), calls=%async_computation.5 | async-start | bytes 2228224 | tf_op jit(solution)/shard_map/reduce_scatter | solution.py:78
Sparse Core Ops, SparseCore 0:
  33.3 20.9 all-reduce.1
  57.4 62.1 all-gather.2
  131.1 10.6 reduce-scatter.2
  144.0 81.9 reduce-scatter.4
where the time goes:
time: 234 us
  waiting for transfers between devices  127 us (54%)
  blocking collectives  41.8 us (18%)
  local copies, waits for them, and re-layouts  28.3 us (12%)
  matrix products  18.2 us (8%)
  between operations  13.3 us (6%)
  other arithmetic  5.64 us (2%)
    reduce_scatter x1, waiting for transfers between devices, local(): moe_share = lax.psum_scatter(own, 'req', scatter_dimension=0, tiled=True)  84.1 us
    all_gather x1, blocking collectives, local(): gates_all = lax.all_gather(gates, 'req', axis=0, tiled=True)  41.8 us
    psum x1, waiting for transfers between devices, local(): summed = lax.psum(partial_value, 'tp')  21.1 us
    slice x1, local copies, waits for them, and re-layouts, attend(): cache_values = kv_cache[:, :, 1].reshape(requests, ctx_len, local_heads, HD)  17.1 us
    reduce_scatter x1, waiting for transfers between devices, local(): lax.psum_scatter(result * weight, 'tp', scatter_dimension=1, tiled=True)  10.8 us
    all_gather x1, waiting for transfers between devices, local(): rows = lax.all_gather(normed, 'req', axis=0, tiled=True)  10.6 us
    slice x1, local copies, waits for them, and re-layouts, local(): gate_up[0, :, 0]  10.4 us
    dot_general x1, matrix products, local(): result = jnp.dot(inner, down_proj[0], preferred_element_type=jnp.float32)  7.25 us
  transfers between devices with their start and end apart: 4, of which 4 were waited for; matrix products, arithmetic and copies ran while one was open for 5% of the time, Pallas kernels for 0%

commit v1 on v0

--- a/solution.py
+++ b/solution.py
@@ -58,7 +58,7 @@
     experts = lax.axis_size("req")
     attended = attend(fresh_qkv, kv_cache, cache_len)
     partial_value = jnp.dot(attended, out_proj, preferred_element_type=jnp.float32)
-    summed = lax.psum(partial_value, "tp")
+    summed = jnp.sum(lax.all_gather(partial_value, "tp"), axis=0)
     hidden = (residual.astype(jnp.float32) + summed).astype(jnp.bfloat16)
     normed = rms_normed(hidden, norm_gain)
     rows = lax.all_gather(normed, "req", axis=0, tiled=True)

time: 234 us -> 214 us (0.915)
  waiting for transfers between devices: 127 us -> 104 us
  blocking collectives: 41.8 us -> 45.4 us
    psum x1 -> x0, waiting for transfers between devices: 21.1 us -> none  [local(): summed = lax.psum(partial_value, 'tp')]
    all_gather x0 -> x1, blocking collectives: none -> 2.39 us  [local(): summed = jnp.sum(lax.all_gather(partial_value, 'tp'), axis=0)]
  transfers between devices with their start and end apart: 4 -> 3, of which waited for: 4 -> 3; matrix products, arithmetic and copies ran while one was open for 5% -> 6% of each run, Pallas kernels for 0% -> 0%
where the time goes in v1:
time: 214 us
  waiting for transfers between devices  104 us (49%)
  blocking collectives  45.4 us (21%)
  local copies, waits for them, and re-layouts  28.3 us (13%)
  matrix products  18.5 us (9%)
  between operations  13.3 us (6%)
  other arithmetic  4.72 us (2%)
    reduce_scatter x1, waiting for transfers between devices, local(): moe_share = lax.psum_scatter(own, 'req', scatter_dimension=0, tiled=True)  84.3 us
    all_gather x1, blocking collectives, local(): gates_all = lax.all_gather(gates, 'req', axis=0, tiled=True)  43 us
    slice x1, local copies, waits for them, and re-layouts, attend(): cache_values = kv_cache[:, :, 1].reshape(requests, ctx_len, local_heads, HD)  17.1 us
    reduce_scatter x1, waiting for transfers between devices, local(): lax.psum_scatter(result * weight, 'tp', scatter_dimension=1, tiled=True)  10.8 us
    slice x1, local copies, waits for them, and re-layouts, local(): gate_up[0, :, 0]  10.4 us
    all_gather x1, waiting for transfers between devices, local(): rows = lax.all_gather(normed, 'req', axis=0, tiled=True)  8.62 us
    dot_general x1, matrix products, local(): result = jnp.dot(inner, down_proj[0], preferred_element_type=jnp.float32)  7.3 us
  transfers between devices with their start and end apart: 3, of which 3 were waited for; matrix products, arithmetic and copies ran while one was open for 6% of the time, Pallas kernels for 0%

profile of v1, /device:TPU:0, one launch (start us, length us, event | category | flops | bytes accessed | tf_op | source)
XLA Modules:
  0.0 214.0 jit_solution(6440824016193036164)
XLA Ops:
  6.5 0.8 iota_compare_fusion.1
  7.4 0.9 convert_bitcast_fusion
  8.4 0.1 fusion.20
  8.5 0.1 copy.30
  8.5 0.1 reshape.55
  8.6 17.1 %slice_reduce_fusion = (bf16[32,24,1024]{2,1,0:T(8,128)(2,1)}, bf16[32,24,1024]{2,1,0:T(8,128)(2,1)S(1)}) fusion(bf16[32,24,2,1024]{3,2,1,0:T(2,128)(2,1)} %param.12), kind=kLoop, calls=%fused_computation.1 | loop fusion | bytes 6291456 | tf_op jit(solution)/shard_map/slice | solution.py:22
  25.7 0.9 fusion.6
  26.7 0.1 copy.26
  26.9 0.1 copy.20
  27.0 0.2 copy.31
  27.2 2.0 fusion.3
  29.2 0.1 fusion.19
  29.3 3.0 %fusion.24 = f32[32,2048]{1,0:T(8,128)S(1)} fusion(bf16[1024,2048]{1,0:T(8,128)(2,1)} %param.14, bf16[4,8,8,128]{3,2,1,0:T(8,128)(2,1)S(1)} %bitcast.86), kind=kOutput, calls=%fused_computation.40 | convolution fusion | flops 134217728 | bytes 4521984 | tf_op jit(solution)/shard_map/dot_general | solution.py:60
  32.4 2.4 %all-gather = f32[64,2048]{1,0:T(8,128)S(1)} all-gather(f32[32,2048]{1,0:T(8,128)S(1)} %fusion.24), channel_id=2, replica_groups=mesh['req'=16,'tp'=2] {'tp'}, dimensions={0}, use_global_device_ids=true | all-gather | bytes 786432 | tf_op jit(solution)/shard_map/all_gather | solution.py:61
  34.8 0.2 fusion.15
  35.0 0.7 fusion.17
  35.7 0.0 all-gather.4.cloned.1.call-update
  35.8 0.0 reduce-scatter.3.cloned.1.call-start
  35.9 1.1 fusion.34
  37.0 43.0 %all-gather.1 = f32[16,32,16]{1,2,0:T(8,128)S(1)} all-gather(f32[1,32,16]{1,2,0:T(8,128)S(1)} %divide_bitcast_fusion), channel_id=1, replica_groups=mesh['req'=16,'tp'=2] {'req'}, dimensions={0}, use_global_device_ids=true | all-gather | bytes 34816 | tf_op jit(solution)/shard_map/all_gather | solution.py:70
  80.1 0.1 reshape.47
  80.2 0.1 select_reduce_fusion
  80.3 10.4 %fusion.33 = (bf16[1,2048,1,512]{3,2,1,0:T(2,128)(2,1)}, bf16[1,2048,1,512]{3,2,1,0:T(2,128)(2,1)}) fusion(bf16[1,2048,2,512]{3,2,1,0:T(2,128)(2,1)} %param.18), kind=kLoop, calls=%fused_computation.61 | loop fusion | bytes 8388608 | tf_op jit(solution)/shard_map/slice | solution.py:73
  90.7 8.6 %all-gather.4.cloned.1.call-done = bf16[512,2048]{1,0:T(8,128)(2,1)} async-done(((bf16[32,2048]{1,0:T(8,128)(2,1)}), bf16[512,2048]{1,0:T(8,128)(2,1)}) %all-gather.4.cloned.1.call-update) | async-done | bytes 2097168 | tf_op jit(solution)/shard_map/all_gather | solution.py:64
  99.3 4.1 %fusion.1 = f32[512,512]{1,0:T(8,128)S(1)} fusion(bf16[512,2048]{1,0:T(8,128)(2,1)} %all-gather.4.cloned.1.call-done, bf16[1,2048,1,512]{3,2,1,0:T(2,128)(2,1)} %get-tuple-element.9), kind=kOutput, calls=%fused_computation.6 | convolution fusion | flops 1073741824 | bytes 5242880 | tf_op jit(solution)/shard_map/dot_general | solution.py:73
  103.4 7.3 %convolution_multiply_fusion = f32[512,2048]{1,0:T(8,128)} fusion(bf16[1,512,2048]{2,1,0:T(8,128)(2,1)S(1)} %copy-done, f32[512]{0:T(512)S(1)} %select_reduce_fusion, bf16[512,2048]{1,0:T(8,128)(2,1)} %all-gather.4.cloned.1.call-done, bf16[1,2048,1,512]{3,2,1,0:T(2,128)(2,1)} %get-tuple-element.10, f32[512,512]{1,0:T(8,128)S(1)} %fusion.1), kind=kOutput, calls=%fused_computation | convolution fusion | flops 2150105088 | bytes 11536384 | tf_op jit(solution)/shard_map/dot_general | solution.py:76
  110.7 0.0 reduce-scatter.3.cloned.1.call-update
  110.8 0.0 reduce-scatter.5.cloned.1.call-start
  110.8 10.8 %reduce-scatter.3.cloned.1.call-done = f32[512,1024]{1,0:T(8,128)} async-done(((f32[512,2048]{1,0:T(8,128)}), f32[512,1024]{1,0:T(8,128)}) %reduce-scatter.3.cloned.1.call-update) | async-done | bytes 2097168 | tf_op jit(solution)/shard_map/reduce_scatter | solution.py:77
  121.6 0.0 reduce-scatter.5.cloned.1.call-update
  121.6 84.3 %reduce-scatter.5.cloned.1.call-done = f32[32,1024]{1,0:T(8,128)} async-done(((f32[512,1024]{1,0:T(8,128)}), f32[32,1024]{1,0:T(8,128)}) %reduce-scatter.5.cloned.1.call-update) | async-done | bytes 131088 | tf_op jit(solution)/shard_map/reduce_scatter | solution.py:78
  205.9 1.5 add_convert_fusion.1
  (26 shorter events, 0.4 us)
Async XLA Ops:
  6.5 96.9 %copy-start = (bf16[1,512,2048]{2,1,0:T(8,128)(2,1)S(1)}, bf16[1,512,2048]{2,1,0:T(8,128)(2,1)}, u32[]{:S(2)}) copy-start(bf16[1,512,2048]{2,1,0:T(8,128)(2,1)} %param.19) | copy-start | bytes 6291460
  6.5 92.8 %all-gather.4.cloned.1.call-start = ((), (), s32[]{:S(2)}) async-start(), calls=%async_computation.2 | async-start | bytes 2228224 | tf_op jit(solution)/shard_map/all_gather | solution.py:64
  29.3 5.5 %copy-start.1 = (bf16[32,2048]{1,0:T(8,128)(2,1)S(1)}, bf16[32,2048]{1,0:T(8,128)(2,1)}, u32[]{:S(2)}) copy-start(bf16[32,2048]{1,0:T(8,128)(2,1)} %param.10) | copy-start | bytes 393220
  32.4 2.6 %copy-start.3 = (f32[2048]{0:T(1024)S(1)}, f32[2048]{0:T(1024)}, u32[]{:S(2)}) copy-start(f32[2048]{0:T(1024)} %param.15) | copy-start | bytes 24580
  32.4 3.5 %copy-start.4 = (s32[32,8]{0,1:T(8,128)S(1)}, s32[32,8]{0,1:T(8,128)}, u32[]{:S(2)}) copy-start(s32[32,8]{0,1:T(8,128)} %param.17) | copy-start | bytes 3076
  32.4 3.5 %copy-start.2 = (f32[2048,16]{0,1:T(8,128)S(1)}, f32[2048,16]{0,1:T(8,128)}, u32[]{:S(2)}) copy-start(f32[2048,16]{0,1:T(8,128)} %param.16) | copy-start | bytes 393220
  35.8 85.8 %reduce-scatter.3.cloned.1.call-start = ((), (), s32[]{:S(2)}) async-start(), calls=%async_computation.3 | async-start | bytes 6291456 | tf_op jit(solution)/shard_map/reduce_scatter | solution.py:77
  110.8 95.1 %reduce-scatter.5.cloned.1.call-start = ((), (), s32[]{:S(2)}) async-start(), calls=%async_computation.4 | async-start | bytes 2228224 | tf_op jit(solution)/shard_map/reduce_scatter | solution.py:78
Sparse Core Ops, SparseCore 0:
  35.9 63.4 all-gather.3
  110.9 10.6 reduce-scatter.2
  124.0 81.8 reduce-scatter.4
